TPU v7x, 128 devices: a whole 4x4x4 slice. The times are simulated.
128 devices in a mesh: depth: 2 (over core), rows: 2 (over x_hi), shots: 32 (over z, y, x_lo).
Axes of the slice: x: 4 (x_hi: 2, x_lo: 2; x = x_hi * 2 + x_lo), y: 4, z: 4, core: 2. Of those that a mesh axis runs over, the one named last changes fastest.
Arguments:
- sources: float32 [2, 2, 1024, 4096], P('depth', None, 'rows', 'shots'), may hold values from -6 to 6
- factor: float32 [2, 2, 1024, 1024], P('depth', None, ('rows', 'shots')), may hold values from -0.09375 to 0.09375
- block_mask: int32 [2, 2, 8, 8], P('depth'), may hold values 0 or 1
- inverse_diagonal: float32 [2, 2, 1024, 1024], P('depth', None, None, 'rows'), may hold values from -1.2 to 1.2, as said below
Outputs:
- solution: float32 [2, 2, 1024, 4096], P('depth', None, 'rows', 'shots')
Inputs may be any that keep to these rules, and one draw needn't show every extreme that they name: Each block inverse_diagonal[d, m] is lower triangular with diagonal entries between 0.8 and 1.2.
All inputs are finite; a program needn't handle non-finite values. No bound on the sum of `block_mask` on one device may be relied on, other than what follows from the above.
Results may differ from a plain program's by a relative error of at most 0.0001.
Values sent between devices are 32-bit elements; how exact they have to be, the bound alone decides.
A program may use at most 64 MiB of HBM per device.

v0:
```python
import jax
import jax.numpy as jnp
from jax import lax
from jax.sharding import PartitionSpec as P


def mask_rows(factor_rows, block_mask, row_start, block_size):
    row_total = factor_rows.shape[1]
    block_count = block_mask.shape[3]
    row_blocks = (row_start + jnp.arange(row_total, dtype=jnp.int32)) // block_size
    row_select = (row_blocks[:, None] == jnp.arange(block_count, dtype=jnp.int32)[None, :]).astype(
        jnp.float32
    )
    row_masks = jnp.einsum("rk,pkc->prc", row_select, block_mask[0].astype(jnp.float32))
    return factor_rows * jnp.repeat(row_masks, block_size, axis=2)


def product(spec, left, right):
    return jnp.einsum(
        spec, left, right, precision=lax.Precision.HIGH, preferred_element_type=jnp.float32
    )


def per_device(sources, factor, block_mask, inverse_diagonal):
    shot_index = lax.axis_index("shots")
    rows_index = lax.axis_index("rows")
    thin_rows = factor.shape[2]
    full_width = factor.shape[3]
    block_size = full_width // block_mask.shape[3]
    row_start = (rows_index * lax.axis_size("shots") + shot_index) * thin_rows
    masked = mask_rows(factor[0], block_mask, row_start, block_size)
    tiles = lax.all_gather(masked, "shots", axis=1, tiled=True)
    low = lax.psum(product("rs,sn->rn", inverse_diagonal[0, 0], sources[0, 0]), "rows")
    update = product("trs,sn->trn", tiles, low)
    own = sources[0, 1] - lax.psum_scatter(update, "depth", scatter_dimension=0, tiled=True)[0]
    high = lax.psum(product("rs,sn->rn", inverse_diagonal[0, 1], own), "rows")
    top = product("sr,sn->rn", inverse_diagonal[0, 1], high)
    tops = lax.all_gather(top[None], "depth", axis=0, tiled=True)
    target = low - lax.psum(product("trs,trn->sn", tiles, tops), "rows")
    bottom = product("sr,sn->rn", inverse_diagonal[0, 0], target)
    return jnp.stack([bottom, top])[None]


def solution(mesh):
    placed = (
        P("depth", None, "rows", "shots"),
        P("depth", None, ("rows", "shots"), None),
        P("depth", None, None, None),
        P("depth", None, None, "rows"),
    )
    return jax.shard_map(
        per_device,
        mesh=mesh,
        in_specs=placed,
        out_specs=P("depth", None, "rows", "shots"),
        check_vma=False,
    )
```

profile of v0, /device:TPU:1, one launch (start us, length us, event | category | flops | bytes accessed | tf_op | source)
XLA Modules:
  0.0 303.1 jit_solution(8039582276913375339)
XLA Ops:
  7.4 0.0 all-reduce.4.cloned.1.call-start
  7.4 3.4 %fusion.6 = f32[1024,128]{1,0:T(8,128)} fusion(f32[1,2,1024,512]{3,2,1,0:T(8,128)} %param.7, f32[1,2,512,128]{3,2,1,0:T(8,128)} %param.4), kind=kOutput, calls=%fused_computation.6 | convolution fusion | flops 402653184 | bytes 2883584 | tf_op jit(solution)/shard_map/rs,sn->rn/dot_general | solution.py:19
  10.8 0.0 copy-start.1
  10.8 0.0 all-reduce.4.cloned.1.call-update
  10.8 0.0 all-gather.3.cloned.1.call-start
  10.8 0.7 convert_bitcast_fusion
  11.6 0.1 copy.5
  11.7 0.1 convolution_bitcast_fusion.1
  11.8 0.1 copy.6
  11.9 0.1 broadcast_in_dim.11
  12.0 1.6 bitcast_multiply_fusion
  13.6 0.0 all-gather.3.cloned.1.call-update
  13.6 0.0 reduce-scatter.2.cloned.1.call-start
  13.7 38.2 %all-reduce.4.cloned.1.call-done = f32[1024,128]{1,0:T(8,128)} async-done(((f32[1024,128]{1,0:T(8,128)}), f32[1024,128]{1,0:T(8,128)}) %all-reduce.4.cloned.1.call-update) | async-done | bytes 524304 | tf_op jit(solution)/shard_map/psum | solution.py:33
  51.8 116.8 %all-gather.3.cloned.1.call-done = f32[2,512,1024]{2,1,0:T(8,128)} async-done(((f32[2,16,1024]{2,1,0:T(8,128)}), f32[2,512,1024]{2,1,0:T(8,128)}) %all-gather.3.cloned.1.call-update) | async-done | bytes 4194320 | tf_op jit(solution)/shard_map/all_gather | solution.py:32
  168.6 4.9 %fusion.18 = f32[2,512,128]{2,1,0:T(8,128)} fusion(f32[2,512,1024]{2,1,0:T(8,128)} %all-gather.3.cloned.1.call-done, f32[1024,128]{1,0:T(8,128)} %all-reduce.4.cloned.1.call-done), kind=kOutput, calls=%fused_computation.17 | convolution fusion | flops 805306368 | bytes 5242880 | tf_op jit(solution)/shard_map/trs,sn->trn/dot_general | solution.py:19
  173.5 0.0 reduce-scatter.2.cloned.1.call-update
  173.5 0.0 all-reduce.6.cloned.1.call-start
  173.6 29.7 %reduce-scatter.2.cloned.1.call-done = f32[1,512,128]{2,1,0:T(8,128)} async-done(((f32[2,512,128]{2,1,0:T(8,128)}), f32[1,512,128]{2,1,0:T(8,128)}) %reduce-scatter.2.cloned.1.call-update) | async-done | bytes 262160 | tf_op jit(solution)/shard_map/reduce_scatter | solution.py:35
  203.3 0.0 copy-done.1
  203.3 3.7 %fusion.12 = f32[1024,128]{0,1:T(8,128)} fusion(f32[1,2,1024,512]{3,2,1,0:T(8,128)} %param.7, f32[1,512,128]{2,1,0:T(8,128)} %reduce-scatter.2.cloned.1.call-done, f32[1,2,512,128]{3,2,1,0:T(8,128)S(1)} %copy-done.1), kind=kOutput, calls=%fused_computation.12 | convolution fusion | flops 402718720 | bytes 3145728 | tf_op jit(solution)/shard_map/rs,sn->rn/dot_general | solution.py:19
  207.0 0.0 all-reduce.6.cloned.1.call-update
  207.0 0.0 all-reduce.8.cloned.1.call-start
  207.0 37.6 %all-reduce.6.cloned.1.call-done = f32[1024,128]{0,1:T(8,128)} async-done(((f32[1024,128]{0,1:T(8,128)}), f32[1024,128]{0,1:T(8,128)}) %all-reduce.6.cloned.1.call-update) | async-done | bytes 524304 | tf_op jit(solution)/shard_map/psum | solution.py:36
  244.7 2.5 fusion
  247.2 0.0 copy-start
  247.2 2.6 all-gather
  249.8 0.2 copy.9
  250.0 6.4 %convolution_bitcast_fusion = f32[1024,128]{1,0:T(8,128)} fusion(f32[2,512,1024]{2,1,0:T(8,128)} %all-gather.3.cloned.1.call-done, f32[2,512,128]{2,1,0:T(8,128)S(1)} %bitcast.63), kind=kOutput, calls=%fused_computation.13 | convolution fusion | flops 805306368 | bytes 5242880 | tf_op jit(solution)/shard_map/trs,trn->sn/dot_general | solution.py:19
  256.4 0.0 all-reduce.8.cloned.1.call-update
  256.4 36.0 %all-reduce.8.cloned.1.call-done = f32[1024,128]{1,0:T(8,128)} async-done(((f32[1024,128]{1,0:T(8,128)}), f32[1024,128]{1,0:T(8,128)}) %all-reduce.8.cloned.1.call-update) | async-done | bytes 524304 | tf_op jit(solution)/shard_map/psum | solution.py:39
  292.4 0.0 copy-done
  292.4 2.5 fusion.15
  295.0 1.0 copy.7
  (3 shorter events, 0.1 us)
Async XLA Ops:
  7.4 44.5 %all-reduce.4.cloned.1.call-start = ((), (), s32[]{:S(2)}) async-start(), calls=%async_computation.1 | async-start | bytes 1048576 | tf_op jit(solution)/shard_map/psum | solution.py:33
  10.8 192.5 %copy-start.1 = (f32[1,2,512,128]{3,2,1,0:T(8,128)S(1)}, f32[1,2,512,128]{3,2,1,0:T(8,128)}, u32[]{:S(2)}) copy-start(f32[1,2,512,128]{3,2,1,0:T(8,128)} %param.4) | copy-start | bytes 1572868
  10.8 157.8 %all-gather.3.cloned.1.call-start = ((), (), s32[]{:S(2)}) async-start(), calls=%async_computation.2 | async-start | bytes 4325376 | tf_op jit(solution)/shard_map/all_gather | solution.py:32
  13.6 189.7 %reduce-scatter.2.cloned.1.call-start = ((), (), s32[]{:S(2)}) async-start(), calls=%async_computation.3 | async-start | bytes 786432 | tf_op jit(solution)/shard_map/reduce_scatter | solution.py:35
  173.5 71.2 %all-reduce.6.cloned.1.call-start = ((), (), s32[]{:S(2)}) async-start(), calls=%async_computation.4 | async-start | bytes 1048576 | tf_op jit(solution)/shard_map/psum | solution.py:36
  207.0 85.4 %all-reduce.8.cloned.1.call-start = ((), (), s32[]{:S(2)}) async-start(), calls=%async_computation.5 | async-start | bytes 1048576 | tf_op jit(solution)/shard_map/psum | solution.py:39
  247.2 45.2 %copy-start = (f32[1024,128]{1,0:T(8,128)S(1)}, f32[1024,128]{1,0:T(8,128)}, u32[]{:S(2)}) copy-start(f32[1024,128]{1,0:T(8,128)} %all-reduce.4.cloned.1.call-done) | copy-start | bytes 1572868
Sparse Core Ops, SparseCore 0:
  10.9 40.8 all-reduce.3
  173.6 29.5 reduce-scatter.1
  207.1 37.5 all-reduce.5
  256.5 35.7 all-reduce.7
Sparse Core Ops, SparseCore 1:
  13.7 154.9 all-gather.2
where the time goes:
time: 303 us
  waiting for transfers between devices  258 us (85%)
  matrix products  23.5 us (8%)
  between operations  14.6 us (5%)
    all_gather x1, waiting for transfers between devices, per_device(): tiles = lax.all_gather(masked, 'shots', axis=1, tiled=True)  117 us
    psum x1, waiting for transfers between devices, per_device(): lax.psum(product('rs,sn->rn', inverse_diagonal[0, 0], sources[0, 0]), 'ro...  38.2 us
    psum x1, waiting for transfers between devices, per_device(): high = lax.psum(product('rs,sn->rn', inverse_diagonal[0, 1], own), 'rows')  37.6 us
    psum x1, waiting for transfers between devices, per_device(): target = low - lax.psum(product('trs,trn->sn', tiles, tops), 'rows')  36 us
    reduce_scatter x1, waiting for transfers between devices, per_device(): lax.psum_scatter(update, 'depth', scatter_dimension=0, tiled=True)[0]  29.7 us
    dot_general x6, matrix products, product(): jnp.einsum(spec, left, right, precision=lax.Precision.HIGH, preferred_ele...  23.4 us
  transfers between devices with their start and end apart: 5, of which 5 were waited for; matrix products, arithmetic and copies ran while one was open for 1% of the time, Pallas kernels for 0%

commit v1 on v0

--- a/solution.py
+++ b/solution.py
@@ -2,6 +2,13 @@
 import jax.numpy as jnp
 from jax import lax
 from jax.sharding import PartitionSpec as P
+
+
+def gather_over(array, name, dim):
+    n_dev = lax.axis_size(name)
+    pieces = jnp.stack([array for _ in range(n_dev)])
+    pieces = lax.all_to_all(pieces, name, split_axis=0, concat_axis=0)
+    return jnp.concatenate(pieces, axis=dim)
 
 
 def mask_rows(factor_rows, block_mask, row_start, block_size):
@@ -29,7 +36,7 @@
     block_size = full_width // block_mask.shape[3]
     row_start = (rows_index * lax.axis_size("shots") + shot_index) * thin_rows
     masked = mask_rows(factor[0], block_mask, row_start, block_size)
-    tiles = lax.all_gather(masked, "shots", axis=1, tiled=True)
+    tiles = gather_over(masked, "shots", 1)
     low = lax.psum(product("rs,sn->rn", inverse_diagonal[0, 0], sources[0, 0]), "rows")
     update = product("trs,sn->trn", tiles, low)
     own = sources[0, 1] - lax.psum_scatter(update, "depth", scatter_dimension=0, tiled=True)[0]

time: 303 us -> 206 us (0.68)
  waiting for transfers between devices: 258 us -> 145 us
  starting transfers between devices: 0.17 us -> 10.2 us
  local copies, waits for them, and re-layouts: 1.48 us -> 8.65 us
    all_gather x1 -> x0, waiting for transfers between devices: 117 us -> none  [per_device(): tiles = lax.all_gather(masked, 'shots', axis=1, tiled=True)]
    all_to_all x0 -> x1, waiting for transfers between devices: none -> 59 us  [gather_over(): pieces = lax.all_to_all(pieces, name, split_axis=0, concat_axis=0)]
    psum x1, waiting for transfers between devices: 38.2 us -> 0.01 us  [per_device(): lax.psum(product('rs,sn->rn', inverse_diagonal[0, 0], sources[0, 0]), 'ro...]
    reduce_scatter x1, waiting for transfers between devices: 29.7 us -> 12.6 us  [per_device(): lax.psum_scatter(update, 'depth', scatter_dimension=0, tiled=True)[0]]
    all_to_all x0 -> x1, starting transfers between devices: none -> 10.1 us  [gather_over(): pieces = lax.all_to_all(pieces, name, split_axis=0, concat_axis=0)]
    reshape x0 -> x1, local copies, waits for them, and re-layouts: none -> 4.71 us  [gather_over(): return jnp.concatenate(pieces, axis=dim)]
  transfers between devices with their start and end apart: 5 -> 5, of which waited for: 5 -> 4; matrix products, arithmetic and copies ran while one was open for 1% -> 4% of each run, Pallas kernels for 0% -> 0%
where the time goes in v1:
time: 206 us; the launch traced here: 205 us
  waiting for transfers between devices  145 us (70%)
  matrix products  23.5 us (11%)
  between operations  13.2 us (6%)
  starting transfers between devices  10.2 us (5%)
  local copies, waits for them, and re-layouts  8.65 us (4%)
  blocking collectives  2.61 us (1%)
    all_to_all x1, waiting for transfers between devices, gather_over(): pieces = lax.all_to_all(pieces, name, split_axis=0, concat_axis=0)  59 us
    psum x1, waiting for transfers between devices, per_device(): high = lax.psum(product('rs,sn->rn', inverse_diagonal[0, 1], own), 'rows')  37.6 us
    psum x1, waiting for transfers between devices, per_device(): target = low - lax.psum(product('trs,trn->sn', tiles, tops), 'rows')  36 us
    dot_general x6, matrix products, product(): jnp.einsum(spec, left, right, precision=lax.Precision.HIGH, preferred_ele...  23.4 us
    reduce_scatter x1, waiting for transfers between devices, per_device(): lax.psum_scatter(update, 'depth', scatter_dimension=0, tiled=True)[0]  12.6 us
    all_to_all x1, starting transfers between devices, gather_over(): pieces = lax.all_to_all(pieces, name, split_axis=0, concat_axis=0)  10.1 us
    reshape x1, local copies, waits for them, and re-layouts, gather_over(): return jnp.concatenate(pieces, axis=dim)  4.71 us
  transfers between devices with their start and end apart: 5, of which 4 were waited for; matrix products, arithmetic and copies ran while one was open for 4% of the time, Pallas kernels for 0%

profile of v1, /device:TPU:1, one launch (start us, length us, event | category | flops | bytes accessed | tf_op | source)
XLA Modules:
  0.0 205.1 jit_solution(12994076606216050788)
XLA Ops:
  6.5 0.7 convert_bitcast_fusion
  7.2 0.1 copy.8
  7.3 0.1 convolution_bitcast_fusion.1
  7.5 0.1 copy.9
  7.5 0.1 broadcast_in_dim.11
  7.7 0.9 multiply_bitcast_fusion
  8.6 2.5 %stack.9 = f32[32,2,16,1024]{3,2,1,0:T(8,128)} broadcast(f32[2,16,1024]{2,1,0:T(8,128)S(1)} %multiply_bitcast_fusion), dimensions={1,2,3} | broadcast | bytes 4325376 | tf_op jit(solution)/shard_map/stack | solution.py:9
  11.1 0.0 copy-start.1
  11.1 10.1 %all-to-all-start = ((f32[32,2,16,1024]{3,2,1,0:T(8,128)}), f32[32,2,16,1024]{3,2,1,0:T(8,128)}, u32[]{:S(2)}, u32[]{:S(2)}) async-start(f32[32,2,16,1024]{3,2,1,0:T(8,128)} %stack.9), calls=%async_computation | async-start | bytes 8388608 | tf_op jit(solution)/shard_map/all_to_all | solution.py:10
  21.1 0.0 all-reduce.4.cloned.1.call-start
  21.2 0.0 copy-done.1
  21.2 3.4 %fusion.6 = f32[1024,128]{1,0:T(8,128)} fusion(f32[1,2,1024,512]{3,2,1,0:T(8,128)} %param.7, f32[1,2,512,128]{3,2,1,0:T(8,128)S(1)} %copy-done.1), kind=kOutput, calls=%fused_computation.6 | convolution fusion | flops 402653184 | bytes 2883584 | tf_op jit(solution)/shard_map/rs,sn->rn/dot_general | solution.py:26
  24.6 0.0 all-reduce.4.cloned.1.call-update
  24.6 0.0 reduce-scatter.2.cloned.1.call-start
  24.6 59.0 %all-to-all-done = f32[32,2,16,1024]{3,2,1,0:T(8,128)} async-done(((f32[32,2,16,1024]{3,2,1,0:T(8,128)}), f32[32,2,16,1024]{3,2,1,0:T(8,128)}, u32[]{:S(2)}, u32[]{:S(2)}) %all-to-all-start) | async-done | bytes 4194336 | tf_op jit(solution)/shard_map/all_to_all | solution.py:10
  83.7 4.7 %copy.10 = f32[2,32,16,1024]{3,2,1,0:T(8,128)} copy(f32[2,32,16,1024]{3,2,0,1:T(8,128)} %bitcast.8) | data formatting | bytes 8388608 | tf_op jit(solution)/shard_map/reshape | solution.py:11
  88.4 0.0 all-reduce.4.cloned.1.call-done
  88.4 4.9 %fusion.18 = f32[2,512,128]{2,1,0:T(8,128)} fusion(f32[2,512,1024]{2,1,0:T(8,128)} %bitcast.63, f32[1024,128]{1,0:T(8,128)} %all-reduce.4.cloned.1.call-done), kind=kOutput, calls=%fused_computation.17 | convolution fusion | flops 805306368 | bytes 5242880 | tf_op jit(solution)/shard_map/trs,sn->trn/dot_general | solution.py:26
  93.3 0.0 reduce-scatter.2.cloned.1.call-update
  93.3 0.0 all-reduce.6.cloned.1.call-start
  93.4 12.6 %reduce-scatter.2.cloned.1.call-done = f32[1,512,128]{2,1,0:T(8,128)} async-done(((f32[2,512,128]{2,1,0:T(8,128)}), f32[1,512,128]{2,1,0:T(8,128)}) %reduce-scatter.2.cloned.1.call-update) | async-done | bytes 262160 | tf_op jit(solution)/shard_map/reduce_scatter | solution.py:42
  105.9 3.7 %fusion.12 = f32[1024,128]{0,1:T(8,128)} fusion(f32[1,2,1024,512]{3,2,1,0:T(8,128)} %param.7, f32[1,512,128]{2,1,0:T(8,128)} %reduce-scatter.2.cloned.1.call-done, f32[1,2,512,128]{3,2,1,0:T(8,128)S(1)} %copy-done.1), kind=kOutput, calls=%fused_computation.12 | convolution fusion | flops 402718720 | bytes 3145728 | tf_op jit(solution)/shard_map/rs,sn->rn/dot_general | solution.py:26
  109.6 0.0 all-reduce.6.cloned.1.call-update
  109.6 0.0 all-reduce.8.cloned.1.call-start
  109.7 37.6 %all-reduce.6.cloned.1.call-done = f32[1024,128]{0,1:T(8,128)} async-done(((f32[1024,128]{0,1:T(8,128)}), f32[1024,128]{0,1:T(8,128)}) %all-reduce.6.cloned.1.call-update) | async-done | bytes 524304 | tf_op jit(solution)/shard_map/psum | solution.py:43
  147.3 2.5 %fusion = f32[128,512]{1,0:T(8,128)S(1)} fusion(f32[1024,128]{0,1:T(8,128)} %all-reduce.6.cloned.1.call-done, f32[1,2,1024,512]{3,2,1,0:T(8,128)} %param.7), kind=kOutput, calls=%fused_computation | convolution fusion | flops 402653184 | bytes 2883584 | tf_op jit(solution)/shard_map/sr,sn->rn/dot_general | solution.py:26
  149.8 0.0 copy-start
  149.8 2.6 %all-gather = f32[1024,128]{0,1:T(8,128)S(1)} all-gather(f32[512,128]{0,1:T(8,128)S(1)} %bitcast.65), channel_id=2, replica_groups=mesh['depth'=2,'rows'=2,'shots'=32] {'depth'}, dimensions={0}, use_global_device_ids=true | all-gather | bytes 786432 | tf_op jit(solution)/shard_map/all_gather | solution.py:45
  152.4 0.2 copy.13
  152.6 6.4 %convolution_bitcast_fusion = f32[1024,128]{1,0:T(8,128)} fusion(f32[2,512,1024]{2,1,0:T(8,128)} %bitcast.64, f32[2,512,128]{2,1,0:T(8,128)S(1)} %bitcast.67), kind=kOutput, calls=%fused_computation.13 | convolution fusion | flops 805306368 | bytes 5242880 | tf_op jit(solution)/shard_map/trs,trn->sn/dot_general | solution.py:26
  159.1 0.0 all-reduce.8.cloned.1.call-update
  159.1 36.0 %all-reduce.8.cloned.1.call-done = f32[1024,128]{1,0:T(8,128)} async-done(((f32[1024,128]{1,0:T(8,128)}), f32[1024,128]{1,0:T(8,128)}) %all-reduce.8.cloned.1.call-update) | async-done | bytes 524304 | tf_op jit(solution)/shard_map/psum | solution.py:46
  195.0 0.0 copy-done
  195.0 2.5 %fusion.15 = f32[1,512,128]{1,2,0:T(8,128)S(1)} fusion(f32[1,2,1024,512]{3,2,1,0:T(8,128)} %param.7, f32[1024,128]{1,0:T(8,128)S(1)} %copy-done, f32[1024,128]{1,0:T(8,128)} %all-reduce.8.cloned.1.call-done), kind=kOutput, calls=%fused_computation.14 | convolution fusion | flops 402784256 | bytes 3407872 | tf_op jit(solution)/shard_map/sr,sn->rn/dot_general | solution.py:26
  197.6 1.0 copy.11
  (3 shorter events, 0.1 us)
Async XLA Ops:
  11.1 10.1 %copy-start.1 = (f32[1,2,512,128]{3,2,1,0:T(8,128)S(1)}, f32[1,2,512,128]{3,2,1,0:T(8,128)}, u32[]{:S(2)}) copy-start(f32[1,2,512,128]{3,2,1,0:T(8,128)} %param.4) | copy-start | bytes 1572868
  11.1 72.6 %all-to-all-start = ((f32[32,2,16,1024]{3,2,1,0:T(8,128)}), f32[32,2,16,1024]{3,2,1,0:T(8,128)}, u32[]{:S(2)}, u32[]{:S(2)}) async-start(f32[32,2,16,1024]{3,2,1,0:T(8,128)} %stack.9), calls=%async_computation | async-start | bytes 8388608 | tf_op jit(solution)/shard_map/all_to_all | solution.py:10
  21.1 67.3 %all-reduce.4.cloned.1.call-start = ((), (), s32[]{:S(2)}) async-start(), calls=%async_computation.2 | async-start | bytes 1048576 | tf_op jit(solution)/shard_map/psum | solution.py:40
  24.6 81.3 %reduce-scatter.2.cloned.1.call-start = ((), (), s32[]{:S(2)}) async-start(), calls=%async_computation.3 | async-start | bytes 786432 | tf_op jit(solution)/shard_map/reduce_scatter | solution.py:42
  93.3 54.0 %all-reduce.6.cloned.1.call-start = ((), (), s32[]{:S(2)}) async-start(), calls=%async_computation.4 | async-start | bytes 1048576 | tf_op jit(solution)/shard_map/psum | solution.py:43
  109.6 85.4 %all-reduce.8.cloned.1.call-start = ((), (), s32[]{:S(2)}) async-start(), calls=%async_computation.5 | async-start | bytes 1048576 | tf_op jit(solution)/shard_map/psum | solution.py:46
  149.8 45.2 %copy-start = (f32[1024,128]{1,0:T(8,128)S(1)}, f32[1024,128]{1,0:T(8,128)}, u32[]{:S(2)}) copy-start(f32[1024,128]{1,0:T(8,128)} %all-reduce.4.cloned.1.call-done) | copy-start | bytes 1572868
Sparse Core Ops, SparseCore 0:
  24.7 50.2 all-reduce.3
  93.4 12.4 reduce-scatter.1
  109.8 37.5 all-reduce.5
  159.2 35.7 all-reduce.7
